TPU v7x, 32 devices: a whole 2x2x4 slice. The times are simulated.
32 devices in a mesh: rows: 8 (over z, x), delay: 4 (over y, core).
Axes of the slice: x: 2, y: 2, z: 4, core: 2. Of those that a mesh axis runs over, the one named last changes fastest.
Arguments:
- excitation: bfloat16 [4, 80, 16384], P(None, None, 'rows'), may hold values from -6 to 6
- past_currents: bfloat16 [4, 80, 16384], P('delay', None, 'rows'), may hold values from -6 to 6
- history_mats: bfloat16 [4, 16384, 16384], P('delay', 'rows'), may hold values from -0.0234375 to 0.0234375
- inverse: bfloat16 [16384, 16384], P('delay', 'rows'), may hold values from -0.046875 to 0.046875
Outputs:
- currents: float32 [4, 80, 16384], P(None, None, ('delay', 'rows'))
All inputs are finite; a program needn't handle non-finite values.
Results may differ from a plain program's by a relative error of at most 0.02.
Values may be sent and summed in bfloat16 or wider, within the bound.
A program may use at most 192 MiB of HBM per device.

v0:
```python
import jax
import jax.numpy as jnp
from jax import lax
from jax.sharding import PartitionSpec as P


def on_device(excitation, past_currents, history_mats, inverse):
    delay_count = lax.axis_size("delay")
    delay_pos = lax.axis_index("delay")
    steps_total = excitation.shape[0]
    local_mat = history_mats[0]
    all_past = lax.all_gather(past_currents, "delay", axis=0, tiled=True)
    all_past = lax.all_gather(all_past, "rows", axis=2, tiled=True)
    window = all_past[::-1]
    delayed_cur = lax.dynamic_index_in_dim(window, delay_count - 1 - delay_pos, 0, keepdims=False)
    results = []
    for step in range(steps_total):
        partial_hist = jnp.dot(delayed_cur, local_mat.T, preferred_element_type=jnp.float32)
        history = lax.psum(partial_hist.astype(jnp.bfloat16), "delay").astype(jnp.float32)
        drive_rows = (excitation[step].astype(jnp.float32) - history).astype(jnp.bfloat16)
        products = lax.dot_general(
            drive_rows, inverse, (((1,), (1,)), ((), ())), preferred_element_type=jnp.float32
        )
        own_piece = lax.psum_scatter(products, "rows", scatter_dimension=1, tiled=True)
        if step + 1 < steps_total:
            group_part = lax.all_gather(own_piece.astype(jnp.bfloat16), "rows", axis=1, tiled=True)
        results.append(own_piece)
        if step + 1 < steps_total:
            newest = lax.all_gather(group_part, "delay", axis=1, tiled=True)
            window = jnp.concatenate([window[1:], newest[None]], axis=0)
            delayed_cur = lax.dynamic_index_in_dim(
                window, delay_count - 1 - delay_pos, 0, keepdims=False
            )
    return jnp.stack(results)


def solution(mesh):
    in_specs = (
        P(None, None, "rows"),
        P("delay", None, "rows"),
        P("delay", "rows", None),
        P("delay", "rows"),
    )
    out_specs = P(None, None, ("delay", "rows"))
    return jax.shard_map(
        on_device, mesh=mesh, in_specs=in_specs, out_specs=out_specs, check_vma=False
    )
```

profile of v0, /device:TPU:12, one launch (start us, length us, event | category | flops | bytes accessed | tf_op | source)
XLA Modules:
  0.0 936.7 jit_solution(7216705492045259500)
XLA Ops:
  7.3 20.0 %all-gather.6.cloned.1.call-done = bf16[4,80,2048]{2,1,0:T(8,128)(2,1)} async-done(((bf16[1,80,2048]{2,1,0:T(8,128)(2,1)}), bf16[4,80,2048]{2,1,0:T(8,128)(2,1)}) %all-gather.6.cloned.1.call-update) | async-done | bytes 1310736 | tf_op jit(solution)/shard_map/all_gather | solution.py:12
  27.4 152.1 %all-gather.8.cloned.1.call-done = bf16[4,80,16384]{2,1,0:T(8,128)(2,1)} async-done(((bf16[4,80,2048]{2,1,0:T(8,128)(2,1)}), bf16[4,80,16384]{2,1,0:T(8,128)(2,1)}) %all-gather.8.cloned.1.call-update) | async-done | bytes 10485776 | tf_op jit(solution)/shard_map/all_gather | solution.py:13
  179.5 9.0 rev.3
  188.5 28.2 %fusion.19 = bf16[80,2048]{1,0:T(8,128)(2,1)} fusion(bf16[1,2048,16384]{2,1,0:T(8,128)(2,1)} %param.6, bf16[4,80,16384]{2,1,0:T(8,128)(2,1)} %rev.3, s32[]{:T(128)S(6)} %select_n.7), kind=kOutput, calls=%fused_computation.22 | convolution fusion | flops 5368872960 | bytes 70057984 | tf_op jit(solution)/shard_map/dot_general | solution.py:18
  216.8 31.5 %all-reduce.5.cloned.1.call-done = bf16[80,2048]{1,0:T(8,128)(2,1)} async-done(((bf16[80,2048]{1,0:T(8,128)(2,1)}), bf16[80,2048]{1,0:T(8,128)(2,1)}) %all-reduce.5.cloned.1.call-update) | async-done | bytes 327696 | tf_op jit(solution)/shard_map/psum | solution.py:19
  248.3 12.3 %fusion.43 = f32[80,4096]{1,0:T(8,128)} fusion(bf16[4096,2048]{1,0:T(8,128)(2,1)} %param.7, bf16[80,2048]{1,0:T(8,128)(2,1)} %all-reduce.5.cloned.1.call-done, bf16[4,80,2048]{2,1,0:T(8,128)(2,1)} %param.4), kind=kOutput, calls=%fused_computation.35 | convolution fusion | flops 1342832640 | bytes 18743296 | tf_op jit(solution)/shard_map/dot_general | solution.py:21
  260.7 65.9 %reduce-scatter.5.cloned.1.call-done = f32[80,512]{1,0:T(8,128)} async-done(((f32[80,4096]{1,0:T(8,128)}), f32[80,512]{1,0:T(8,128)}) %reduce-scatter.5.cloned.1.call-update) | async-done | bytes 163856 | tf_op jit(solution)/shard_map/reduce_scatter | solution.py:24
  326.6 0.9 convert_element_type.76
  327.5 31.4 %all_gather.26 = bf16[80,4096]{1,0:T(8,128)(2,1)} all-gather(bf16[80,512]{1,0:T(8,128)(2,1)S(1)} %convert_element_type.76), channel_id=1, replica_groups=mesh['rows'=8,'delay'=4] {'rows'}, dimensions={1}, use_global_device_ids=true | all-gather | bytes 737280 | tf_op jit(solution)/shard_map/all_gather | solution.py:26
  359.0 7.2 slice.32
  366.1 7.9 slice.27
  374.0 11.3 %all-gather.10.cloned.1.call-done = bf16[80,16384]{1,0:T(8,128)(2,1)} async-done(((bf16[80,4096]{1,0:T(8,128)(2,1)}), bf16[80,16384]{1,0:T(8,128)(2,1)}) %all-gather.10.cloned.1.call-update) | async-done | bytes 2621456 | tf_op jit(solution)/shard_map/all_gather | solution.py:29
  385.3 28.3 %fusion.24 = bf16[80,2048]{1,0:T(8,128)(2,1)} fusion(bf16[1,2048,16384]{2,1,0:T(8,128)(2,1)} %param.6, s32[]{:T(128)S(6)} %select_n.7, bf16[3,80,16384]{2,1,0:T(8,128)(2,1)} %slice.27, bf16[1,80,16384]{2,1,0:T(8,128)(2,1)} %bitcast.72), kind=kOutput, calls=%fused_computation.23 | convolution fusion | flops 5370183680 | bytes 77922304 | tf_op jit(solution)/shard_map/dot_general | solution.py:18
  413.9 32.2 %all-reduce.7.cloned.1.call-done = bf16[80,2048]{1,0:T(8,128)(2,1)} async-done(((bf16[80,2048]{1,0:T(8,128)(2,1)}), bf16[80,2048]{1,0:T(8,128)(2,1)}) %all-reduce.7.cloned.1.call-update) | async-done | bytes 327696 | tf_op jit(solution)/shard_map/psum | solution.py:19
  446.1 12.2 %fusion.45 = f32[80,4096]{1,0:T(8,128)} fusion(bf16[4096,2048]{1,0:T(8,128)(2,1)} %param.7, bf16[80,2048]{1,0:T(8,128)(2,1)} %all-reduce.7.cloned.1.call-done, bf16[4,80,2048]{2,1,0:T(8,128)(2,1)} %param.4), kind=kOutput, calls=%fused_computation.36 | convolution fusion | flops 1342832640 | bytes 18743296 | tf_op jit(solution)/shard_map/dot_general | solution.py:21
  458.4 65.9 %reduce-scatter.7.cloned.1.call-done = f32[80,512]{1,0:T(8,128)} async-done(((f32[80,4096]{1,0:T(8,128)}), f32[80,512]{1,0:T(8,128)}) %reduce-scatter.7.cloned.1.call-update) | async-done | bytes 163856 | tf_op jit(solution)/shard_map/reduce_scatter | solution.py:24
  525.2 31.3 %all_gather.28 = bf16[80,4096]{1,0:T(8,128)(2,1)} all-gather(bf16[80,512]{1,0:T(8,128)(2,1)S(1)} %convert_element_type.82), channel_id=1, replica_groups=mesh['rows'=8,'delay'=4] {'rows'}, dimensions={1}, use_global_device_ids=true | all-gather | bytes 737280 | tf_op jit(solution)/shard_map/all_gather | solution.py:26
  556.5 26.5 %all-gather.12.cloned.1.call-done = bf16[80,16384]{1,0:T(8,128)(2,1)} async-done(((bf16[80,4096]{1,0:T(8,128)(2,1)}), bf16[80,16384]{1,0:T(8,128)(2,1)}) %all-gather.12.cloned.1.call-update) | async-done | bytes 2621456 | tf_op jit(solution)/shard_map/all_gather | solution.py:29
  583.0 8.7 fusion.8
  591.8 28.3 %fusion.29 = bf16[80,2048]{1,0:T(8,128)(2,1)} fusion(bf16[1,2048,16384]{2,1,0:T(8,128)(2,1)} %param.6, bf16[4,80,16384]{2,1,0:T(8,128)(2,1)} %fusion.8, s32[]{:T(128)S(6)} %select_n.7), kind=kOutput, calls=%fused_computation.24 | convolution fusion | flops 5368872960 | bytes 70057984 | tf_op jit(solution)/shard_map/dot_general | solution.py:18
  620.2 32.3 %all-reduce.9.cloned.1.call-done = bf16[80,2048]{1,0:T(8,128)(2,1)} async-done(((bf16[80,2048]{1,0:T(8,128)(2,1)}), bf16[80,2048]{1,0:T(8,128)(2,1)}) %all-reduce.9.cloned.1.call-update) | async-done | bytes 327696 | tf_op jit(solution)/shard_map/psum | solution.py:19
  652.5 12.2 %fusion.47 = f32[80,4096]{1,0:T(8,128)} fusion(bf16[4096,2048]{1,0:T(8,128)(2,1)} %param.7, bf16[80,2048]{1,0:T(8,128)(2,1)} %all-reduce.9.cloned.1.call-done, bf16[4,80,2048]{2,1,0:T(8,128)(2,1)S(1)} %copy-done.1), kind=kOutput, calls=%fused_computation.37 | convolution fusion | flops 1342832640 | bytes 18743296 | tf_op jit(solution)/shard_map/dot_general | solution.py:21
  664.8 65.9 %reduce-scatter.9.cloned.1.call-done = f32[80,512]{1,0:T(8,128)} async-done(((f32[80,4096]{1,0:T(8,128)}), f32[80,512]{1,0:T(8,128)}) %reduce-scatter.9.cloned.1.call-update) | async-done | bytes 163856 | tf_op jit(solution)/shard_map/reduce_scatter | solution.py:24
  730.7 0.9 convert_element_type.88
  731.6 31.3 %all_gather.30 = bf16[80,4096]{1,0:T(8,128)(2,1)} all-gather(bf16[80,512]{1,0:T(8,128)(2,1)S(1)} %convert_element_type.88), channel_id=1, replica_groups=mesh['rows'=8,'delay'=4] {'rows'}, dimensions={1}, use_global_device_ids=true | all-gather | bytes 737280 | tf_op jit(solution)/shard_map/all_gather | solution.py:26
  763.2 7.1 slice.33
  770.4 19.1 %all-gather.14.cloned.1.call-done = bf16[80,16384]{1,0:T(8,128)(2,1)} async-done(((bf16[80,4096]{1,0:T(8,128)(2,1)}), bf16[80,16384]{1,0:T(8,128)(2,1)}) %all-gather.14.cloned.1.call-update) | async-done | bytes 2621456 | tf_op jit(solution)/shard_map/all_gather | solution.py:29
  789.5 28.3 %fusion.34 = bf16[80,2048]{1,0:T(8,128)(2,1)} fusion(bf16[1,2048,16384]{2,1,0:T(8,128)(2,1)} %param.6, s32[]{:T(128)S(6)} %select_n.7, bf16[3,80,16384]{2,1,0:T(8,128)(2,1)} %slice.33, bf16[1,80,16384]{2,1,0:T(8,128)(2,1)} %bitcast.74), kind=kOutput, calls=%fused_computation.25 | convolution fusion | flops 5370183680 | bytes 77922304 | tf_op jit(solution)/shard_map/dot_general | solution.py:18
  817.9 32.4 %all-reduce.11.cloned.1.call-done = bf16[80,2048]{1,0:T(8,128)(2,1)} async-done(((bf16[80,2048]{1,0:T(8,128)(2,1)}), bf16[80,2048]{1,0:T(8,128)(2,1)}) %all-reduce.11.cloned.1.call-update) | async-done | bytes 327696 | tf_op jit(solution)/shard_map/psum | solution.py:19
  850.3 12.2 %fusion.49 = f32[80,4096]{1,0:T(8,128)} fusion(bf16[4096,2048]{1,0:T(8,128)(2,1)} %param.7, bf16[80,2048]{1,0:T(8,128)(2,1)} %all-reduce.11.cloned.1.call-done, bf16[4,80,2048]{2,1,0:T(8,128)(2,1)S(1)} %copy-done.1), kind=kOutput, calls=%fused_computation.38 | convolution fusion | flops 1342832640 | bytes 18743296 | tf_op jit(solution)/shard_map/dot_general | solution.py:21
  862.5 65.9 %reduce-scatter.11.cloned.1.call-done = f32[80,512]{1,0:T(8,128)} async-done(((f32[80,4096]{1,0:T(8,128)}), f32[80,512]{1,0:T(8,128)}) %reduce-scatter.11.cloned.1.call-update) | async-done | bytes 163856 | tf_op jit(solution)/shard_map/reduce_scatter | solution.py:24
  928.3 1.8 pad_maximum_fusion.1
  (37 shorter events, 2.8 us)
Async XLA Ops:
  6.5 20.8 %all-gather.6.cloned.1.call-start = ((), (), s32[]{:S(2)}) async-start(), calls=%async_computation.4 | async-start | bytes 1638400 | tf_op jit(solution)/shard_map/all_gather | solution.py:12
  7.3 172.2 %all-gather.8.cloned.1.call-start = ((), (), s32[]{:S(2)}) async-start(), calls=%async_computation.5 | async-start | bytes 11796480 | tf_op jit(solution)/shard_map/all_gather | solution.py:13
  27.4 221.0 %all-reduce.5.cloned.1.call-start = ((), (), s32[]{:S(2)}) async-start(), calls=%async_computation.6 | async-start | bytes 655360 | tf_op jit(solution)/shard_map/psum | solution.py:19
  216.8 109.8 %reduce-scatter.5.cloned.1.call-start = ((), (), s32[]{:S(2)}) async-start(), calls=%async_computation.7 | async-start | bytes 1474560 | tf_op jit(solution)/shard_map/reduce_scatter | solution.py:24
  260.6 124.7 %all-gather.10.cloned.1.call-start = ((), (), s32[]{:S(2)}) async-start(), calls=%async_computation.8 | async-start | bytes 3276800 | tf_op jit(solution)/shard_map/all_gather | solution.py:29
  358.9 87.2 %all-reduce.7.cloned.1.call-start = ((), (), s32[]{:S(2)}) async-start(), calls=%async_computation.9 | async-start | bytes 655360 | tf_op jit(solution)/shard_map/psum | solution.py:19
  413.6 169.4 %copy-start = (bf16[80,16384]{1,0:T(8,128)(2,1)S(1)}, bf16[80,16384]{1,0:T(8,128)(2,1)}, u32[]{:S(2)}) copy-start(bf16[80,16384]{1,0:T(8,128)(2,1)} %all-gather.10.cloned.1.call-done) | copy-start | bytes 7864324
  413.6 110.6 %reduce-scatter.7.cloned.1.call-start = ((), (), s32[]{:S(2)}) async-start(), calls=%async_computation.10 | async-start | bytes 1474560 | tf_op jit(solution)/shard_map/reduce_scatter | solution.py:24
  458.3 124.7 %all-gather.12.cloned.1.call-start = ((), (), s32[]{:S(2)}) async-start(), calls=%async_computation.11 | async-start | bytes 3276800 | tf_op jit(solution)/shard_map/all_gather | solution.py:29
  556.5 96.0 %all-reduce.9.cloned.1.call-start = ((), (), s32[]{:S(2)}) async-start(), calls=%async_computation.12 | async-start | bytes 655360 | tf_op jit(solution)/shard_map/psum | solution.py:19
  591.8 60.8 %copy-start.1 = (bf16[4,80,2048]{2,1,0:T(8,128)(2,1)S(1)}, bf16[4,80,2048]{2,1,0:T(8,128)(2,1)}, u32[]{:S(2)}) copy-start(bf16[4,80,2048]{2,1,0:T(8,128)(2,1)} %param.4) | copy-start | bytes 3932164
  620.1 110.6 %reduce-scatter.9.cloned.1.call-start = ((), (), s32[]{:S(2)}) async-start(), calls=%async_computation.13 | async-start | bytes 1474560 | tf_op jit(solution)/shard_map/reduce_scatter | solution.py:24
  664.7 124.8 %all-gather.14.cloned.1.call-start = ((), (), s32[]{:S(2)}) async-start(), calls=%async_computation.14 | async-start | bytes 3276800 | tf_op jit(solution)/shard_map/all_gather | solution.py:29
  763.0 87.3 %all-reduce.11.cloned.1.call-start = ((), (), s32[]{:S(2)}) async-start(), calls=%async_computation.15 | async-start | bytes 655360 | tf_op jit(solution)/shard_map/psum | solution.py:19
  817.8 110.5 %copy-start.2 = (f32[80,512]{1,0:T(8,128)S(1)}, f32[80,512]{1,0:T(8,128)}, u32[]{:S(2)}) copy-start(f32[80,512]{1,0:T(8,128)} %reduce-scatter.5.cloned.1.call-done) | copy-start | bytes 491524
  817.8 110.5 %copy-start.3 = (f32[80,512]{1,0:T(8,128)S(1)}, f32[80,512]{1,0:T(8,128)}, u32[]{:S(2)}) copy-start(f32[80,512]{1,0:T(8,128)} %reduce-scatter.7.cloned.1.call-done) | copy-start | bytes 491524
  817.8 110.5 %copy-start.4 = (f32[80,512]{1,0:T(8,128)S(1)}, f32[80,512]{1,0:T(8,128)}, u32[]{:S(2)}) copy-start(f32[80,512]{1,0:T(8,128)} %reduce-scatter.9.cloned.1.call-done) | copy-start | bytes 491524
  817.8 110.5 %reduce-scatter.11.cloned.1.call-start = ((), (), s32[]{:S(2)}) async-start(), calls=%async_computation.16 | async-start | bytes 1474560 | tf_op jit(solution)/shard_map/reduce_scatter | solution.py:24
Sparse Core Ops, SparseCore 0:
  8.9 18.3 all-gather.5
  29.5 149.9 all-gather.7
  216.9 31.3 all-reduce.4
  260.8 65.7 reduce-scatter.4
  359.0 26.2 all-gather.9
  413.7 32.2 all-reduce.6
  458.4 65.7 reduce-scatter.6
  556.6 26.3 all-gather.11
  620.2 32.2 all-reduce.8
  664.8 65.7 reduce-scatter.8
  763.1 26.3 all-gather.13
  817.9 32.2 all-reduce.10
  862.6 65.6 reduce-scatter.10
where the time goes:
time: 939 us; the launch traced here: 937 us
  waiting for transfers between devices  622 us (66%)
  matrix products  162 us (17%)
  blocking collectives  94 us (10%)
  local copies, waits for them, and re-layouts  31.3 us (3%)
  other arithmetic  13.3 us (1%)
  between operations  13.3 us (1%)
    reduce_scatter x4, waiting for transfers between devices, on_device(): lax.psum_scatter(products, 'rows', scatter_dimension=1, tiled=True)  264 us
    all_gather x1, waiting for transfers between devices, on_device(): all_past = lax.all_gather(all_past, 'rows', axis=2, tiled=True)  152 us
    psum x4, waiting for transfers between devices, on_device(): lax.psum(partial_hist.astype(jnp.bfloat16), 'delay').astype(jnp.float32)  128 us
    dot_general x4, matrix products, on_device(): jnp.dot(delayed_cur, local_mat.T, preferred_element_type=jnp.float32)  113 us
    all_gather x3, blocking collectives, on_device(): lax.all_gather(own_piece.astype(jnp.bfloat16), 'rows', axis=1, tiled=True)  94 us
    all_gather x3, waiting for transfers between devices, on_device(): newest = lax.all_gather(group_part, 'delay', axis=1, tiled=True)  56.9 us
    dot_general x4, matrix products, on_device(): lax.dot_general(drive_rows, inverse, (((1,), (1,)), ((), ())), preferred_...  48.9 us
    slice x3, local copies, waits for them, and re-layouts, on_device(): window = jnp.concatenate([window[1:], newest[None]], axis=0)  22.2 us
  transfers between devices with their start and end apart: 13, of which 13 were waited for; matrix products, arithmetic and copies ran while one was open for 2% of the time, Pallas kernels for 0%

commit v1 on v0

--- a/solution.py
+++ b/solution.py
@@ -1,6 +1,10 @@
+import functools
+
 import jax
 import jax.numpy as jnp
 from jax import lax
+from jax.experimental import pallas as pl
+from jax.experimental.pallas import tpu as pltpu
 from jax.sharding import PartitionSpec as P
 
 
@@ -34,6 +38,273 @@
     return jnp.stack(results)
 
 
+MESH = pl.DeviceIdType.MESH
+F32, BF16 = jnp.float32, jnp.bfloat16
+SLOTS = 12
+
+
+def dot_rows(a, b):
+    return lax.dot_general(a, b, (((1,), (1,)), ((), ())), preferred_element_type=F32)
+
+
+def march(R, D, S, exc, past, mats, inv_hbm, out, xs, hbuf, inv, total, parts, part_out, drive,
+          red_out, red_in, newest, hsem, inv_sem, blk_send, blk_recv, blk_fwd, pc_send, pc_recv,
+          pc_fwd, sh_send, sh_recv, part_send, part_recv, drv_send, drv_recv, red_send, red_recv):
+    r, d = lax.axis_index("rows"), lax.axis_index("delay")
+    Z, NP = R // 2, R * D
+    E, W = total.shape
+    P = W // D
+    z, x = r // 2, lax.rem(r, 2)
+    mate = r + 1 - 2 * x
+    half = W // 4
+
+    def lane(o):
+        return lax.rem(z + o, Z) * 2 + x
+
+    def source(o):
+        return lax.rem(z + o, Z) * 2 + jnp.where(o < Z, x, 1 - x)
+
+    def remote(src, dst, send, recv, row, delay):
+        return pltpu.make_async_remote_copy(
+            src_ref=src, dst_ref=dst, send_sem=send, recv_sem=recv,
+            device_id={"rows": row, "delay": delay}, device_id_type=MESH)
+
+    def chunk_copy(t):
+        s, k = t // NP, lax.rem(t, NP)
+        src, e = source(k // D), lax.rem(k, D)
+        q = jnp.where(s == 0, src * D + e, e * R + src)
+        slot = lax.rem(t, SLOTS)
+        return pltpu.make_async_copy(
+            mats.at[:, pl.ds(pl.multiple_of(q * P, P), P)], hbuf.at[slot], hsem.at[slot])
+
+    def prefetch(t, c):
+        chunk_copy(t).start()
+        return c
+
+    lax.fori_loop(0, SLOTS, prefetch, 0)
+    inv_copy = pltpu.make_async_copy(inv_hbm, inv, inv_sem)
+    inv_copy.start()
+
+    barrier = pltpu.get_barrier_semaphore()
+
+    def greet(row, delay):
+        pl.semaphore_signal(barrier, inc=1, device_id={"rows": row, "delay": delay}, device_id_type=MESH)
+
+    for o in range(1, R):
+        greet(lax.rem(r + o, R), d)
+    for o in range(1, D):
+        greet(r, lax.rem(d + o, D))
+
+    @pl.when(d == 0)
+    def _():
+        for o in range(1, Z):
+            for e in range(1, D):
+                greet(lane(o), e)
+        pl.semaphore_wait(barrier, R - 1 + D - 1 + (Z - 1) * (D - 1))
+
+    @pl.when(d != 0)
+    def _():
+        for o in range(1, Z):
+            greet(lane(o), 0)
+        pl.semaphore_wait(barrier, R - 1 + D - 1 + Z - 1)
+
+    def block(row):
+        return xs.at[0, pl.ds(row * D, D)]
+
+    def multiply(s, k, q):
+        t = s * NP + k
+        slot = lax.rem(t, SLOTS)
+        chunk_copy(t).wait()
+        piece = xs[s, q]
+        for i in range(4):
+            at = pl.ds(i * half, half)
+            total[:, at] += dot_rows(piece, hbuf[slot, at, :])
+
+        @pl.when(t + SLOTS < S * NP)
+        def _():
+            chunk_copy(t + SLOTS).start()
+
+    for e in range(D):
+        xs[0, r * D + e] = past[:, e * P:(e + 1) * P]
+    for o in range(1, Z):
+        remote(block(r), block(r), blk_send.at[o - 1], blk_recv.at[r], lane(o), d).start()
+
+    for s in range(S):
+        total[...] = jnp.zeros_like(total)
+        if s == 0:
+            def by_block(o, c):
+                src = source(o)
+
+                @pl.when(o != 0)
+                def _():
+                    remote(block(src), block(src), blk_fwd.at[0], blk_recv.at[src], mate, d).wait_recv()
+
+                @pl.when(o < Z)
+                def _():
+                    remote(block(src), block(src), blk_fwd.at[o], blk_recv.at[src], mate, d).start()
+
+                def by_piece(e, c):
+                    multiply(0, o * D + e, src * D + e)
+                    return c
+
+                return lax.fori_loop(0, D, by_piece, c)
+
+            lax.fori_loop(0, R, by_block, 0)
+            for o in range(1, Z):
+                remote(block(r), block(r), blk_send.at[o - 1], blk_recv.at[r], lane(o), d).wait_send()
+            for o in range(Z):
+                remote(block(r), block(r), blk_fwd.at[o], blk_recv.at[r], mate, d).wait_send()
+        else:
+            @pl.when(d != 0)
+            def _():
+                remote(xs.at[s - 1], xs.at[s], sh_send.at[s - 1], sh_recv.at[s - 1], r, d - 1).wait_recv()
+
+            if s < S - 1:
+                @pl.when(jnp.logical_and(d != 0, d < D - 1))
+                def _():
+                    remote(xs.at[s], xs.at[s + 1], sh_send.at[s], sh_recv.at[s], r, d + 1).start()
+
+            def by_piece(k, c):
+                o, e = k // D, lax.rem(k, D)
+                q = e * R + source(o)
+                piece = xs.at[s, q]
+
+                @pl.when(jnp.logical_and(d == 0, k != 0))
+                def _():
+                    remote(piece, piece, pc_fwd.at[0], pc_recv.at[s - 1, q], mate, 0).wait_recv()
+
+                @pl.when(jnp.logical_and(d == 0, o < Z))
+                def _():
+                    remote(piece, piece, pc_fwd.at[k], pc_recv.at[s - 1, q], mate, 0).start()
+
+                multiply(s, k, q)
+                return c
+
+            lax.fori_loop(0, NP, by_piece, 0)
+
+            @pl.when(d == 0)
+            def _():
+                def sent(k, c):
+                    remote(xs.at[s, 0], xs.at[s, 0], pc_fwd.at[k], pc_recv.at[s - 1, 0], mate, 0).wait_send()
+                    return c
+
+                lax.fori_loop(0, Z * D, sent, 0)
+
+        if s < S - 1:
+            first = (d == 0) if s > 0 else (d < D - 1)
+
+            @pl.when(first)
+            def _():
+                remote(xs.at[s], xs.at[s + 1], sh_send.at[s], sh_recv.at[s], r, d + 1).start()
+
+        @pl.when(d != 0)
+        def _():
+            part_out[...] = total[...].astype(BF16)
+            up = remote(part_out, parts.at[d - 1], part_send, part_recv.at[d - 1], r, 0)
+            up.start()
+            up.wait_send()
+            remote(drive, drive, drv_send.at[0], drv_recv, r, 0).wait_recv()
+
+        @pl.when(d == 0)
+        def _():
+            for e in range(D - 1):
+                remote(part_out, parts.at[e], part_send, part_recv.at[e], r, e + 1).wait_recv()
+            history = total[...]
+            for e in range(D - 1):
+                history = history + parts[e].astype(F32)
+            drive[...] = (exc[s].astype(F32) - history).astype(BF16)
+            downs = [remote(drive, drive, drv_send.at[e - 1], drv_recv, r, e) for e in range(D - 1, 0, -1)]
+            for down in downs:
+                down.start()
+
+        if s == 0:
+            inv_copy.wait()
+
+        def by_row(o, c):
+            to = lax.rem(r + o + 1, R)
+            red_out[o] = dot_rows(
+                drive[...], inv[pl.ds(pl.multiple_of(to * P, P), P), :]).astype(BF16)
+            remote(red_out.at[o], red_in.at[o], red_send.at[o], red_recv.at[o], to, d).start()
+            return c
+
+        lax.fori_loop(0, R - 1, by_row, 0)
+        current = dot_rows(drive[...], inv[pl.ds(pl.multiple_of(r * P, P), P), :])
+        for o in range(R - 1):
+            remote(red_out.at[o], red_in.at[o], red_send.at[o], red_recv.at[o], r, d).wait()
+            current = current + red_in[o].astype(F32)
+        out[s] = current
+
+        @pl.when(d == 0)
+        def _():
+            for e in range(D - 1, 0, -1):
+                remote(drive, drive, drv_send.at[e - 1], drv_recv, r, e).wait_send()
+
+        if s < S - 1:
+            mine = d * R + r
+            newest[s] = current.astype(BF16)
+            for o in list(range(1, Z)) + [0]:
+                send = remote(newest.at[s], xs.at[s + 1, mine], pc_send.at[s, o],
+                              pc_recv.at[s, mine], lane(o), 0)
+                if o == 0:
+                    pl.when(d != 0)(send.start)
+                else:
+                    send.start()
+
+            @pl.when(d == 0)
+            def _():
+                xs[s + 1, mine] = current.astype(BF16)
+
+    for s in range(S - 1):
+        for o in range(Z):
+            send = remote(newest.at[s], newest.at[s], pc_send.at[s, o], pc_recv.at[s, 0], r, 0)
+            if o == 0:
+                pl.when(d != 0)(send.wait_send)
+            else:
+                send.wait_send()
+
+        @pl.when(d < D - 1)
+        def _():
+            remote(xs.at[s], xs.at[s + 1], sh_send.at[s], sh_recv.at[s], r, d + 1).wait_send()
+
+
+def in_one_kernel(excitation, past_currents, history_mats, inverse):
+    R, D = lax.axis_size("rows"), lax.axis_size("delay")
+    S, E, W = excitation.shape
+    N, P, Z = W * R, W // D, R // 2
+    NP = R * D
+    dma = pltpu.SemaphoreType.DMA
+    vmem, anywhere = pl.BlockSpec(memory_space=pltpu.VMEM), pl.BlockSpec(memory_space=pl.ANY)
+    return pl.pallas_call(
+        functools.partial(march, R, D, S),
+        out_shape=jax.ShapeDtypeStruct((S, E, P), F32),
+        in_specs=[vmem, vmem, anywhere, anywhere],
+        out_specs=vmem,
+        scratch_shapes=[
+            pltpu.VMEM((S, NP, E, P), BF16),
+            pltpu.VMEM((SLOTS, W, P), BF16),
+            pltpu.VMEM((N // D, W), BF16),
+            pltpu.VMEM((E, W), F32),
+            pltpu.VMEM((D - 1, E, W), BF16),
+            pltpu.VMEM((E, W), BF16),
+            pltpu.VMEM((E, W), BF16),
+            pltpu.VMEM((R - 1, E, P), BF16),
+            pltpu.VMEM((R - 1, E, P), BF16),
+            pltpu.VMEM((S - 1, E, P), BF16),
+            dma((SLOTS,)), dma(()),
+            dma((Z - 1,)), dma((R,)), dma((Z,)),
+            dma((S - 1, Z)), dma((S - 1, NP)), dma((Z * D,)),
+            dma((S - 1,)), dma((S - 1,)),
+            dma(()), dma((D - 1,)),
+            dma((D - 1,)), dma(()),
+            dma((R - 1,)), dma((R - 1,)),
+        ],
+        compiler_params=pltpu.CompilerParams(
+            collective_id=0, has_side_effects=True, vmem_limit_bytes=62 * 2**20),
+        cost_estimate=pl.CostEstimate(
+            flops=2 * S * E * (N * W + N // D * W), bytes_accessed=2 * S * N * W, transcendentals=0),
+    )(excitation, past_currents[0], history_mats[0], inverse)
+
+
 def solution(mesh):
     in_specs = (
         P(None, None, "rows"),
@@ -42,6 +313,14 @@
         P("delay", "rows"),
     )
     out_specs = P(None, None, ("delay", "rows"))
+    rows, delays = mesh.shape["rows"], mesh.shape["delay"]
+
+    def body(excitation, past_currents, history_mats, inverse):
+        steps, _, width = excitation.shape
+        fits = width % (delays * 128) == 0 and rows % 2 == 0 and rows <= 8
+        run = in_one_kernel if fits else on_device
+        return run(excitation, past_currents, history_mats, inverse)
+
     return jax.shard_map(
-        on_device, mesh=mesh, in_specs=in_specs, out_specs=out_specs, check_vma=False
+        body, mesh=mesh, in_specs=in_specs, out_specs=out_specs, check_vma=False
     )

time: 939 us -> 266 us (0.28)
  waiting for transfers between devices: 622 us -> 0 us
  Pallas kernels: 0 us -> 263 us
  matrix products: 162 us -> 0 us
  blocking collectives: 94 us -> 0 us
  local copies, waits for them, and re-layouts: 31.3 us -> 1.97 us
  other arithmetic: 13.3 us -> 0 us
  between operations: 13.3 us -> 0.01 us
    reduce_scatter x4 -> x0, waiting for transfers between devices: 264 us -> none  [on_device(): lax.psum_scatter(products, 'rows', scatter_dimension=1, tiled=True)]
    pallas_call x0 -> x1, Pallas kernels: none -> 263 us  [in_one_kernel(): pl.pallas_call(functools.partial(march, R, D, S), out_shape=jax.ShapeDtyp...]
    all_gather x5 -> x0, waiting for transfers between devices: 229 us -> none  [the longest x1 152 us: on_device(): all_past = lax.all_gather(all_past, 'rows', axis=2, tiled=True)]
    dot_general x8 -> x0, matrix products: 162 us -> none  [the longest x4 113 us: on_device(): jnp.dot(delayed_cur, local_mat.T, preferred_element_type=jnp.float32)]
    psum x4 -> x0, waiting for transfers between devices: 128 us -> none  [on_device(): lax.psum(partial_hist.astype(jnp.bfloat16), 'delay').astype(jnp.float32)]
    all_gather x3 -> x0, blocking collectives: 94 us -> none  [on_device(): lax.all_gather(own_piece.astype(jnp.bfloat16), 'rows', axis=1, tiled=True)]
    slice x3 -> x0, local copies, waits for them, and re-layouts: 22.2 us -> none  [on_device(): window = jnp.concatenate([window[1:], newest[None]], axis=0)]
  transfers between devices with their start and end apart: 13 -> 0, of which waited for: 13 -> 0; matrix products, arithmetic and copies ran while one was open for 2% -> 0% of each run, Pallas kernels for 0% -> 0%
where the time goes in v1:
time: 266 us; the launch traced here: 265 us
  Pallas kernels  263 us (99%)
    pallas_call x1, Pallas kernels, in_one_kernel(): pl.pallas_call(functools.partial(march, R, D, S), out_shape=jax.ShapeDtyp...  263 us

profile of v1, /device:TPU:12, one launch (start us, length us, event | category | flops | bytes accessed | tf_op | source)
XLA Modules:
  0.0 265.5 jit_solution(6185182992961657361)
XLA Ops:
  0.0 263.5 %shard_map.46 = f32[4,80,512]{2,1,0:T(8,128)} custom-call(bf16[4,80,2048]{2,1,0:T(8,128)(2,1)} %exc.1, bf16[80,2048]{1,0:T(8,128)(2,1)} %bitcast.2, bf16[2048,16384]{1,0:T(8,128)(2,1)} %bitcast.1.mats, bf16[4096,2048]{1,0:T(8,128)(2,1)} %inv_hbm.1), custom_call_target="tpu_custom_call" | custom-call | flops 26843545600 | bytes 268435456 | tf_op jit(solution)/shard_map/pallas_call | solution.py:277
  263.5 2.0 copy.6

commit v2 on v1

--- a/solution.py
+++ b/solution.py
@@ -49,7 +49,7 @@
 
 def march(R, D, S, exc, past, mats, inv_hbm, out, xs, hbuf, inv, total, parts, part_out, drive,
           red_out, red_in, newest, hsem, inv_sem, blk_send, blk_recv, blk_fwd, pc_send, pc_recv,
-          pc_fwd, sh_send, sh_recv, part_send, part_recv, drv_send, drv_recv, red_send, red_recv):
+          pc_fwd, sh_send, sh_recv, shb_send, shb_recv, part_send, part_recv, drv_send, drv_recv, red_send, red_recv):
     r, d = lax.axis_index("rows"), lax.axis_index("delay")
     Z, NP = R // 2, R * D
     E, W = total.shape
@@ -110,6 +110,10 @@
 
     def block(row):
         return xs.at[0, pl.ds(row * D, D)]
+
+    def shift_block(o):
+        src = source(o)
+        return remote(block(src), xs.at[1, pl.ds(src * D, D)], shb_send.at[o], shb_recv.at[o], r, d + 1)
 
     def multiply(s, k, q):
         t = s * NP + k
@@ -143,6 +147,10 @@
                 def _():
                     remote(block(src), block(src), blk_fwd.at[o], blk_recv.at[src], mate, d).start()
 
+                @pl.when(d < D - 1)
+                def _():
+                    shift_block(o).start()
+
                 def by_piece(e, c):
                     multiply(0, o * D + e, src * D + e)
                     return c
@@ -157,7 +165,11 @@
         else:
             @pl.when(d != 0)
             def _():
-                remote(xs.at[s - 1], xs.at[s], sh_send.at[s - 1], sh_recv.at[s - 1], r, d - 1).wait_recv()
+                if s == 1:
+                    for o in range(R):
+                        shift_block(o).wait_recv()
+                else:
+                    remote(xs.at[s - 1], xs.at[s], sh_send.at[s - 1], sh_recv.at[s - 1], r, d - 1).wait_recv()
 
             if s < S - 1:
                 @pl.when(jnp.logical_and(d != 0, d < D - 1))
@@ -190,13 +202,6 @@
 
                 lax.fori_loop(0, Z * D, sent, 0)
 
-        if s < S - 1:
-            first = (d == 0) if s > 0 else (d < D - 1)
-
-            @pl.when(first)
-            def _():
-                remote(xs.at[s], xs.at[s + 1], sh_send.at[s], sh_recv.at[s], r, d + 1).start()
-
         @pl.when(d != 0)
         def _():
             part_out[...] = total[...].astype(BF16)
@@ -204,6 +209,10 @@
             up.start()
             up.wait_send()
             remote(drive, drive, drv_send.at[0], drv_recv, r, 0).wait_recv()
+
+        @pl.when(d == 2)
+        def _():
+            remote(drive, drive, drv_send.at[0], drv_recv, r, 3).start()
 
         @pl.when(d == 0)
         def _():
@@ -213,7 +222,7 @@
             for e in range(D - 1):
                 history = history + parts[e].astype(F32)
             drive[...] = (exc[s].astype(F32) - history).astype(BF16)
-            downs = [remote(drive, drive, drv_send.at[e - 1], drv_recv, r, e) for e in range(D - 1, 0, -1)]
+            downs = [remote(drive, drive, drv_send.at[e - 1], drv_recv, r, e) for e in (2, 1)]
             for down in downs:
                 down.start()
 
@@ -228,6 +237,11 @@
             return c
 
         lax.fori_loop(0, R - 1, by_row, 0)
+        if 0 < s < S - 1:
+            @pl.when(d == 0)
+            def _():
+                remote(xs.at[s], xs.at[s + 1], sh_send.at[s], sh_recv.at[s], r, d + 1).start()
+
         current = dot_rows(drive[...], inv[pl.ds(pl.multiple_of(r * P, P), P), :])
         for o in range(R - 1):
             remote(red_out.at[o], red_in.at[o], red_send.at[o], red_recv.at[o], r, d).wait()
@@ -236,8 +250,12 @@
 
         @pl.when(d == 0)
         def _():
-            for e in range(D - 1, 0, -1):
+            for e in (2, 1):
                 remote(drive, drive, drv_send.at[e - 1], drv_recv, r, e).wait_send()
+
+        @pl.when(d == 2)
+        def _():
+            remote(drive, drive, drv_send.at[0], drv_recv, r, 3).wait_send()
 
         if s < S - 1:
             mine = d * R + r
@@ -264,7 +282,11 @@
 
         @pl.when(d < D - 1)
         def _():
-            remote(xs.at[s], xs.at[s + 1], sh_send.at[s], sh_recv.at[s], r, d + 1).wait_send()
+            if s == 0:
+                for o in range(R):
+                    shift_block(o).wait_send()
+            else:
+                remote(xs.at[s], xs.at[s + 1], sh_send.at[s], sh_recv.at[s], r, d + 1).wait_send()
 
 
 def in_one_kernel(excitation, past_currents, history_mats, inverse):
@@ -293,7 +315,7 @@
             dma((SLOTS,)), dma(()),
             dma((Z - 1,)), dma((R,)), dma((Z,)),
             dma((S - 1, Z)), dma((S - 1, NP)), dma((Z * D,)),
-            dma((S - 1,)), dma((S - 1,)),
+            dma((S - 1,)), dma((S - 1,)), dma((R,)), dma((R,)),
             dma(()), dma((D - 1,)),
             dma((D - 1,)), dma(()),
             dma((R - 1,)), dma((R - 1,)),
@@ -317,7 +339,7 @@
 
     def body(excitation, past_currents, history_mats, inverse):
         steps, _, width = excitation.shape
-        fits = width % (delays * 128) == 0 and rows % 2 == 0 and rows <= 8
+        fits = width % (delays * 128) == 0 and rows % 2 == 0 and rows <= 8 and delays == 4
         run = in_one_kernel if fits else on_device
         return run(excitation, past_currents, history_mats, inverse)
 

time: 266 us -> 264 us (level)
  Pallas kernels: 263 us -> 260 us
    pallas_call x1, Pallas kernels: 263 us -> 260 us  [in_one_kernel(): pl.pallas_call(functools.partial(march, R, D, S), out_shape=jax.ShapeDtyp...]
where the time goes in v2:
time: 264 us; the launch traced here: 262 us
  Pallas kernels  260 us (98%)
    pallas_call x1, Pallas kernels, in_one_kernel(): pl.pallas_call(functools.partial(march, R, D, S), out_shape=jax.ShapeDtyp...  260 us

profile of v2, /device:TPU:12, one launch (start us, length us, event | category | flops | bytes accessed | tf_op | source)
XLA Modules:
  0.0 261.5 jit_solution(14575815605472009016)
XLA Ops:
  0.0 259.5 %shard_map.46 = f32[4,80,512]{2,1,0:T(8,128)} custom-call(bf16[4,80,2048]{2,1,0:T(8,128)(2,1)} %exc.1, bf16[80,2048]{1,0:T(8,128)(2,1)} %bitcast.2, bf16[2048,16384]{1,0:T(8,128)(2,1)} %bitcast.1.mats, bf16[4096,2048]{1,0:T(8,128)(2,1)} %inv_hbm.1), custom_call_target="tpu_custom_call" | custom-call | flops 26843545600 | bytes 268435456 | tf_op jit(solution)/shard_map/pallas_call | solution.py:299
  259.5 2.0 copy.6
